TPU v7x, 256 devices: a whole 4x4x8 slice. The times are simulated.
256 devices in a mesh: dp: 32 (over y, z_lo, core), pos: 8 (over z_hi, x).
Axes of the slice: x: 4, y: 4, z: 8 (z_hi: 2, z_lo: 4; z = z_hi * 4 + z_lo), core: 2. Of those that a mesh axis runs over, the one named last changes fastest.
Arguments:
- inputs: bfloat16 [64, 2048, 512], P('dp', 'pos'), may hold values from -6 to 6
- pre_act: bfloat16 [64, 2048, 512], P('dp', 'pos'), may hold values from -6 to 6
- grad_out: bfloat16 [64, 2048, 512], P('dp', 'pos'), may hold values from -6 to 6
- weight: bfloat16 [512, 9, 512], P(('dp', 'pos')), may hold values from -0.09375 to 0.09375
Outputs:
- grad_input: bfloat16 [64, 2048, 512], P('dp', 'pos')
- grad_weight: float32 [512, 9, 512], P(('dp', 'pos'))
All inputs are finite; a program needn't handle non-finite values.
Results may differ from a plain program's by a relative error of at most 0.005.
Values may be sent and summed in bfloat16 or wider, within the bound.
A program may use at most 128 MiB of HBM per device.

v0:
```python
import jax
import jax.numpy as jnp
from jax import lax
from jax.sharding import PartitionSpec as P

K = 9


def padded_2(block, sides, width):
    for axis, dim in sides:
        count = lax.axis_size(axis)
        forward = [(i, i + 1) for i in range(count - 1)]
        backward = [(target, source) for source, target in forward]
        low = lax.ppermute(
            lax.slice_in_dim(block, block.shape[dim] - width, None, axis=dim), axis, forward
        )
        high = lax.ppermute(lax.slice_in_dim(block, 0, width, axis=dim), axis, backward)
        block = jnp.concatenate([low, block, high], axis=dim)
    return block


def partner(block, axis, distance):
    count = lax.axis_size(axis)
    route = []
    for low in range(count):
        high = low | 1 << distance
        if high != low and high < count:
            route += [(low, high), (high, low)]
    return lax.ppermute(block, axis, route)


def gelu_slope(values):
    cdf = 0.5 * (1.0 + lax.erf(values * 0.7071067811865476))
    return cdf + values * jnp.exp(-0.5 * values * values) * 0.3989422804014327


def on_device(inputs, pre_act, grad_out, weight):
    seq_count, length, chan_width = inputs.shape
    half_width = (K - 1) // 2
    grad_pre = (grad_out.astype(jnp.float32) * gelu_slope(pre_act.astype(jnp.float32))).astype(
        jnp.bfloat16
    )
    stacked = jnp.stack([inputs, grad_pre])
    padded = padded_2(stacked, (("pos", 2),), half_width)
    whole = lax.all_gather(weight, ("dp", "pos"), axis=0, tiled=True)
    bit_count = lax.axis_size("pos").bit_length() - 1
    mirrored = padded
    for bit_num in range(bit_count):
        mirrored = partner(mirrored, "pos", bit_num)
    reverse = jnp.flip(mirrored, axis=(2, 3))
    both_inputs = jnp.stack([padded[0], reverse[0]])
    both_grads = jnp.stack([padded[1], reverse[1]])
    total = jnp.zeros((2, seq_count, length, chan_width), jnp.float32)
    for offset in range(K):
        begin = K - 1 - offset
        total = total + jnp.einsum(
            "bsto,io->bsti",
            both_grads[:, :, begin : begin + length],
            whole[:, offset, :],
            preferred_element_type=jnp.float32,
        )
    returned = total[1]
    for bit_num in range(bit_count):
        returned = partner(returned, "pos", bit_num)
    grad_input = (total[0] + jnp.flip(returned, axis=(1, 2))).astype(jnp.bfloat16)
    centre_grads = both_grads[:, :, half_width : half_width + length]
    full_terms = jnp.stack(
        [
            jnp.einsum(
                "bsti,bsto->io",
                both_inputs[:, :, offset : offset + length],
                centre_grads,
                preferred_element_type=jnp.float32,
            )
            for offset in range(K)
        ],
        axis=1,
    )
    grad_weight = lax.psum_scatter(full_terms, ("dp", "pos"), scatter_dimension=0, tiled=True)
    return (grad_input, grad_weight)


def solution(mesh):
    placed = (
        P("dp", "pos", None),
        P("dp", "pos", None),
        P("dp", "pos", None),
        P(("dp", "pos"), None, None),
    )
    return jax.shard_map(
        on_device,
        mesh=mesh,
        in_specs=placed,
        out_specs=(P("dp", "pos", None), P(("dp", "pos"), None, None)),
        check_vma=False,
    )
```

profile of v0, /device:TPU:97, one launch (start us, length us, event | category | flops | bytes accessed | tf_op | source)
XLA Modules:
  0.0 1133.1 jit_solution(16518667106808815034)
XLA Ops:
  7.2 0.0 copy-start
  7.2 0.0 all-gather.2.cloned.1.call-start
  7.2 1.4 copy.15
  8.6 0.0 all-gather.2.cloned.1.call-update
  8.6 0.0 all-reduce.3.cloned.1.call-start
  8.7 1.7 fusion.60
  10.4 0.8 pad_maximum_fusion.6
  11.1 3.1 collective-permute-start
  14.3 1.3 collective-permute-start.1
  15.6 0.0 collective-permute-done
  15.6 3.2 collective-permute-done.1
  18.8 0.0 copy-done
  18.8 0.3 pad_maximum_fusion
  19.0 1.3 collective-permute-start.2
  20.3 22.0 %collective-permute-done.2 = bf16[2,2,264,512]{3,2,1,0:T(8,128)(2,1)S(1)} collective-permute-done((bf16[2,2,264,512]{3,2,1,0:T(8,128)(2,1)S(1)}, bf16[2,2,264,512]{3,2,1,0:T(8,128)(2,1)S(1)}, u32[]{:S(2)}, u32[]{:S(2)}) %collective-permute-start.2) | collective-permute-done | bytes 1081376 | tf_op jit(solution)/shard_map/ppermute | solution.py:29
  42.4 13.7 %collective-permute-start.3 = (bf16[2,2,264,512]{3,2,1,0:T(8,128)(2,1)S(1)}, bf16[2,2,264,512]{3,2,1,0:T(8,128)(2,1)S(1)}, u32[]{:S(2)}, u32[]{:S(2)}) collective-permute-start(bf16[2,2,264,512]{3,2,1,0:T(8,128)(2,1)S(1)} %collective-permute-done.2), channel_id=1, source_target_pairs={{0,2},{2,0},{1,3},{3,1},{4,6},{6,4},{5,7},{7,5},{8,10},{10,8},{9,1... | collective-permute-start | bytes 3244040 | tf_op jit(solution)/shard_map/ppermute | solution.py:29
  56.1 23.8 %collective-permute-done.3 = bf16[2,2,264,512]{3,2,1,0:T(8,128)(2,1)S(1)} collective-permute-done((bf16[2,2,264,512]{3,2,1,0:T(8,128)(2,1)S(1)}, bf16[2,2,264,512]{3,2,1,0:T(8,128)(2,1)S(1)}, u32[]{:S(2)}, u32[]{:S(2)}) %collective-permute-start.3) | collective-permute-done | bytes 1081376 | tf_op jit(solution)/shard_map/ppermute | solution.py:29
  79.9 0.0 collective-permute-start.4
  79.9 0.1 fusion.80
  80.0 34.6 %collective-permute-done.4 = bf16[2,2,264,512]{3,2,1,0:T(8,128)(2,1)S(1)} collective-permute-done((bf16[2,2,264,512]{3,2,1,0:T(8,128)(2,1)S(1)}, bf16[2,2,264,512]{3,2,1,0:T(8,128)(2,1)S(1)}, u32[]{:S(2)}, u32[]{:S(2)}) %collective-permute-start.4) | collective-permute-done | bytes 1081376 | tf_op jit(solution)/shard_map/ppermute | solution.py:29
  114.6 0.1 fusion.79
  114.7 3.1 slice.116
  117.8 3.1 slice.139
  121.0 0.3 fusion.47
  121.3 1.7 fusion.8
  123.0 1.7 fusion.7
  124.8 1.8 fusion.6
  126.6 1.8 fusion.5
  128.4 1.7 fusion.4
  130.1 1.7 fusion.3
  131.8 1.8 fusion.2
  133.6 1.7 fusion.1
  135.3 1.7 fusion
  137.1 0.0 all-reduce.3.cloned.1.call-update
  137.1 619.3 %all-gather.2.cloned.1.call-done = bf16[512,9,512]{2,1,0:T(8,128)(2,1)} async-done(((bf16[2,9,512]{2,1,0:T(8,128)(2,1)}), bf16[512,9,512]{2,1,0:T(8,128)(2,1)}) %all-gather.2.cloned.1.call-update) | async-done | bytes 4718608 | tf_op jit(solution)/shard_map/all_gather | solution.py:45
  756.4 19.3 %fusion.78 = (bf16[512,1,512]{2,1,0:T(2,128)(2,1)S(1)}, bf16[512,1,512]{2,1,0:T(2,128)(2,1)S(1)}, bf16[512,1,512]{2,1,0:T(2,128)(2,1)S(1)}, bf16[512,1,512]{2,1,...) fusion(bf16[512,9,512]{2,1,0:T(8,128)(2,1)} %all-gather.2.clone, ...), kind=kLoop, calls=%fused_computation.126 | loop fusion | bytes 9437184 | tf_op jit(solution)/shard_map/slice | solution.py:59
  775.8 0.7 fusion.36
  776.5 0.8 fusion.39
  777.3 0.8 fusion.42
  778.0 0.7 fusion.45
  778.8 0.8 fusion.49
  779.5 0.8 fusion.52
  780.3 0.8 fusion.33
  781.1 0.7 fusion.59
  781.8 1.6 add_add_fusion
  783.4 0.1 slice_bitcast_fusion
  783.5 37.9 %collective-permute-start.5 = (f32[2,256,512]{2,1,0:T(8,128)S(1)}, f32[2,256,512]{2,1,0:T(8,128)S(1)}, u32[]{:S(2)}, u32[]{:S(2)}) collective-permute-start(f32[2,256,512]{2,1,0:T(8,128)S(1)} %slice_bitcast_fusion), channel_id=1, source_target_pairs={{0,1},{1,0},{2,3},{3,2},{4,5},{5,4},{6,7},{7,6},{8,9},{9,8},{10,11... | collective-permute-start | bytes 3145736 | tf_op jit(solution)/shard_map/ppermute | solution.py:29
  821.4 25.9 %collective-permute-done.5 = f32[2,256,512]{2,1,0:T(8,128)S(1)} collective-permute-done((f32[2,256,512]{2,1,0:T(8,128)S(1)}, f32[2,256,512]{2,1,0:T(8,128)S(1)}, u32[]{:S(2)}, u32[]{:S(2)}) %collective-permute-start.5) | collective-permute-done | bytes 1048608 | tf_op jit(solution)/shard_map/ppermute | solution.py:29
  847.3 1.3 collective-permute-start.6
  848.5 24.0 %collective-permute-done.6 = f32[2,256,512]{2,1,0:T(8,128)S(1)} collective-permute-done((f32[2,256,512]{2,1,0:T(8,128)S(1)}, f32[2,256,512]{2,1,0:T(8,128)S(1)}, u32[]{:S(2)}, u32[]{:S(2)}) %collective-permute-start.6) | collective-permute-done | bytes 1048608 | tf_op jit(solution)/shard_map/ppermute | solution.py:29
  872.5 0.0 collective-permute-start.7
  872.5 243.8 %all-reduce.3.cloned.1.call-done = f32[512,9,512]{2,0,1:T(8,128)} async-done(((f32[512,9,512]{2,0,1:T(8,128)}), f32[512,9,512]{2,0,1:T(8,128)}) %all-reduce.3.cloned.1.call-update) | async-done | bytes 9437200
  1116.3 1.5 constant_dynamic-slice_fusion
  1117.8 0.0 collective-permute-done.7
  1117.8 7.5 rev.6
  1125.3 1.0 fusion.56
Async XLA Ops:
  7.2 11.6 %copy-start = (bf16[2,256,512]{2,1,0:T(8,128)(2,1)S(1)}, bf16[2,256,512]{2,1,0:T(8,128)(2,1)}, u32[]{:S(2)}) copy-start(bf16[2,256,512]{2,1,0:T(8,128)(2,1)} %param.4) | copy-start | bytes 1572868
  7.2 749.3 %all-gather.2.cloned.1.call-start = ((), (), s32[]{:S(2)}) async-start(), calls=%async_computation | async-start | bytes 8421376 | tf_op jit(solution)/shard_map/all_gather | solution.py:45
  8.6 1107.7 %all-reduce.3.cloned.1.call-start = ((), (), s32[]{:S(2)}) async-start(), calls=%async_computation.1 | async-start | bytes 18874368
  11.1 4.4 collective-permute-start
  14.3 4.5 collective-permute-start.1
  19.0 23.3 %collective-permute-start.2 = (bf16[2,2,264,512]{3,2,1,0:T(8,128)(2,1)S(1)}, bf16[2,2,264,512]{3,2,1,0:T(8,128)(2,1)S(1)}, u32[]{:S(2)}, u32[]{:S(2)}) collective-permute-start(bf16[2,2,264,512]{3,2,1,0:T(8,128)(2,1)S(1)} %pad_maximum_fusion), channel_id=1, source_target_pairs={{0,1},{1,0},{2,3},{3,2},{4,5},{5,4},{6,7},{7,6},{8,9},{9,8},{10,11... | collective-permute-start | bytes 3244040 | tf_op jit(solution)/shard_map/ppermute | solution.py:29
  42.4 37.5 %collective-permute-start.3 = (bf16[2,2,264,512]{3,2,1,0:T(8,128)(2,1)S(1)}, bf16[2,2,264,512]{3,2,1,0:T(8,128)(2,1)S(1)}, u32[]{:S(2)}, u32[]{:S(2)}) collective-permute-start(bf16[2,2,264,512]{3,2,1,0:T(8,128)(2,1)S(1)} %collective-permute-done.2), channel_id=1, source_target_pairs={{0,2},{2,0},{1,3},{3,1},{4,6},{6,4},{5,7},{7,5},{8,10},{10,8},{9,1... | collective-permute-start | bytes 3244040 | tf_op jit(solution)/shard_map/ppermute | solution.py:29
  79.9 34.7 %collective-permute-start.4 = (bf16[2,2,264,512]{3,2,1,0:T(8,128)(2,1)S(1)}, bf16[2,2,264,512]{3,2,1,0:T(8,128)(2,1)S(1)}, u32[]{:S(2)}, u32[]{:S(2)}) collective-permute-start(bf16[2,2,264,512]{3,2,1,0:T(8,128)(2,1)S(1)} %collective-permute-done.3), channel_id=1, source_target_pairs={{0,4},{4,0},{1,5},{5,1},{2,6},{6,2},{3,7},{7,3},{8,12},{12,8},{9,1... | collective-permute-start | bytes 3244040 | tf_op jit(solution)/shard_map/ppermute | solution.py:29
  783.5 63.8 %collective-permute-start.5 = (f32[2,256,512]{2,1,0:T(8,128)S(1)}, f32[2,256,512]{2,1,0:T(8,128)S(1)}, u32[]{:S(2)}, u32[]{:S(2)}) collective-permute-start(f32[2,256,512]{2,1,0:T(8,128)S(1)} %slice_bitcast_fusion), channel_id=1, source_target_pairs={{0,1},{1,0},{2,3},{3,2},{4,5},{5,4},{6,7},{7,6},{8,9},{9,8},{10,11... | collective-permute-start | bytes 3145736 | tf_op jit(solution)/shard_map/ppermute | solution.py:29
  847.3 25.2 %collective-permute-start.6 = (f32[2,256,512]{2,1,0:T(8,128)S(1)}, f32[2,256,512]{2,1,0:T(8,128)S(1)}, u32[]{:S(2)}, u32[]{:S(2)}) collective-permute-start(f32[2,256,512]{2,1,0:T(8,128)S(1)} %collective-permute-done.5), channel_id=1, source_target_pairs={{0,2},{2,0},{1,3},{3,1},{4,6},{6,4},{5,7},{7,5},{8,10},{10,8},{9,1... | collective-permute-start | bytes 3145736 | tf_op jit(solution)/shard_map/ppermute | solution.py:29
  872.5 245.3 %collective-permute-start.7 = (f32[2,256,512]{2,1,0:T(8,128)S(1)}, f32[2,256,512]{2,1,0:T(8,128)}, u32[]{:S(2)}, u32[]{:S(2)}) collective-permute-start(f32[2,256,512]{2,1,0:T(8,128)S(1)} %collective-permute-done.6), channel_id=1, source_target_pairs={{0,4},{4,0},{1,5},{5,1},{2,6},{6,2},{3,7},{7,3},{8,12},{12,8},{9,1... | collective-permute-start | bytes 3145736 | tf_op jit(solution)/shard_map/ppermute | solution.py:29
Sparse Core Ops, SparseCore 0:
  10.5 745.9 all-gather.1
  762.0 354.2 all-reduce.2
where the time goes:
time: 1130 us
  waiting for transfers between devices  997 us (88%)
  starting transfers between devices  58.7 us (5%)
  local copies, waits for them, and re-layouts  36.3 us (3%)
  matrix products  23.3 us (2%)
  between operations  14.2 us (1%)
    all_gather x1, waiting for transfers between devices, on_device(): whole = lax.all_gather(weight, ('dp', 'pos'), axis=0, tiled=True)  619 us
    unnamed x3, waiting for transfers between devices  244 us
    ppermute x6, waiting for transfers between devices, partner(): return lax.ppermute(block, axis, route)  130 us
    ppermute x6, starting transfers between devices, partner(): return lax.ppermute(block, axis, route)  54.2 us
  transfers between devices with their start and end apart: 10, of which 8 were waited for; matrix products, arithmetic and copies ran while one was open for 5% of the time, Pallas kernels for 0%

commit v1 on v0

--- a/solution.py
+++ b/solution.py
@@ -42,7 +42,10 @@
     )
     stacked = jnp.stack([inputs, grad_pre])
     padded = padded_2(stacked, (("pos", 2),), half_width)
-    whole = lax.all_gather(weight, ("dp", "pos"), axis=0, tiled=True)
+    whole = jnp.concatenate(
+        lax.all_to_all(jnp.stack([weight] * lax.axis_size(("dp", "pos"))), ("dp", "pos"), 0, 0),
+        axis=0,
+    )
     bit_count = lax.axis_size("pos").bit_length() - 1
     mirrored = padded
     for bit_num in range(bit_count):

time: 1130 us -> 613 us (0.54)
  waiting for transfers between devices: 997 us -> 438 us
  starting transfers between devices: 58.7 us -> 94.9 us
    all_gather x1 -> x0, waiting for transfers between devices: 619 us -> none  [on_device(): whole = lax.all_gather(weight, ('dp', 'pos'), axis=0, tiled=True)]
    unnamed x3 -> x2, waiting for transfers between devices: 244 us -> 278 us
    ppermute x6, waiting for transfers between devices: 130 us -> 153 us  [partner(): return lax.ppermute(block, axis, route)]
    ppermute x6, starting transfers between devices: 54.2 us -> 75.3 us  [partner(): return lax.ppermute(block, axis, route)]
    slice x1 -> x0, local copies, waits for them, and re-layouts: 19.3 us -> none  [on_device(): whole[:, offset, :]]
    all_to_all x0 -> x1, starting transfers between devices: none -> 15.2 us  [on_device(): lax.all_to_all(jnp.stack([weight] * lax.axis_size(('dp', 'pos'))), ('dp',...]
  transfers between devices with their start and end apart: 10 -> 10, of which waited for: 8 -> 8; matrix products, arithmetic and copies ran while one was open for 5% -> 8% of each run, Pallas kernels for 0% -> 0%
where the time goes in v1:
time: 613 us; the launch traced here: 612 us
  waiting for transfers between devices  438 us (71%)
  starting transfers between devices  94.9 us (15%)
  local copies, waits for them, and re-layouts  37.2 us (6%)
  matrix products  25.2 us (4%)
  between operations  14.2 us (2%)
    unnamed x2, waiting for transfers between devices  278 us
    ppermute x6, waiting for transfers between devices, partner(): return lax.ppermute(block, axis, route)  153 us
    ppermute x6, starting transfers between devices, partner(): return lax.ppermute(block, axis, route)  75.3 us
    dot_general x9, matrix products, on_device(): jnp.einsum('bsti,bsto->io', both_inputs[:, :, offset:offset + length], ce...  15.8 us
    all_to_all x1, starting transfers between devices, on_device(): lax.all_to_all(jnp.stack([weight] * lax.axis_size(('dp', 'pos'))), ('dp',...  15.2 us
  transfers between devices with their start and end apart: 10, of which 8 were waited for; matrix products, arithmetic and copies ran while one was open for 8% of the time, Pallas kernels for 0%

profile of v1, /device:TPU:97, one launch (start us, length us, event | category | flops | bytes accessed | tf_op | source)
XLA Modules:
  0.0 611.8 jit_solution(17168105684709080449)
XLA Ops:
  7.2 5.4 stack.36
  12.5 0.0 copy-start.2
  12.5 0.0 copy-start.3
  12.5 0.0 copy-start.1
  12.5 15.2 %all-to-all-start = ((bf16[256,2,9,512]{3,1,2,0:T(2,128)(2,1)}), bf16[256,2,9,512]{3,1,2,0:T(2,128)(2,1)}, u32[]{:S(2)}, u32[]{:S(2)}) async-start(bf16[256,2,9,512]{3,1,2,0:T(2,128)(2,1)} %stack.36), calls=%async_computation | async-start | bytes 9437184 | tf_op jit(solution)/shard_map/all_to_all | solution.py:46
  27.8 0.0 all-reduce.3.cloned.1.call-start
  27.8 0.0 copy-done.2
  27.8 0.0 copy-done.3
  27.8 0.5 fusion.60
  28.3 0.0 copy-done.1
  28.4 3.1 collective-permute-start
  31.5 1.3 collective-permute-start.1
  32.8 2.5 collective-permute-done
  35.3 4.2 collective-permute-done.1
  39.5 0.3 pad_maximum_fusion
  39.8 0.1 collective-permute-start.2
  39.9 44.0 %collective-permute-done.2 = bf16[2,2,264,512]{3,2,1,0:T(8,128)(2,1)S(1)} collective-permute-done((bf16[2,2,264,512]{3,2,1,0:T(8,128)(2,1)S(1)}, bf16[2,2,264,512]{3,2,1,0:T(8,128)(2,1)S(1)}, u32[]{:S(2)}, u32[]{:S(2)}) %collective-permute-start.2) | collective-permute-done | bytes 1081376 | tf_op jit(solution)/shard_map/ppermute | solution.py:29
  83.8 74.0 %collective-permute-start.3 = (bf16[2,2,264,512]{3,2,1,0:T(8,128)(2,1)S(1)}, bf16[2,2,264,512]{3,2,1,0:T(8,128)(2,1)S(1)}, u32[]{:S(2)}, u32[]{:S(2)}) collective-permute-start(bf16[2,2,264,512]{3,2,1,0:T(8,128)(2,1)S(1)} %collective-permute-done.2), channel_id=1, source_target_pairs={{0,2},{2,0},{1,3},{3,1},{4,6},{6,4},{5,7},{7,5},{8,10},{10,8},{9,1... | collective-permute-start | bytes 3244040 | tf_op jit(solution)/shard_map/ppermute | solution.py:29
  157.8 23.1 %collective-permute-done.3 = bf16[2,2,264,512]{3,2,1,0:T(8,128)(2,1)S(1)} collective-permute-done((bf16[2,2,264,512]{3,2,1,0:T(8,128)(2,1)S(1)}, bf16[2,2,264,512]{3,2,1,0:T(8,128)(2,1)S(1)}, u32[]{:S(2)}, u32[]{:S(2)}) %collective-permute-start.3) | collective-permute-done | bytes 1081376 | tf_op jit(solution)/shard_map/ppermute | solution.py:29
  180.9 0.6 collective-permute-start.4
  181.5 0.1 fusion.79
  181.5 27.2 %collective-permute-done.4 = bf16[2,2,264,512]{3,2,1,0:T(8,128)(2,1)S(1)} collective-permute-done((bf16[2,2,264,512]{3,2,1,0:T(8,128)(2,1)S(1)}, bf16[2,2,264,512]{3,2,1,0:T(8,128)(2,1)S(1)}, u32[]{:S(2)}, u32[]{:S(2)}) %collective-permute-start.4) | collective-permute-done | bytes 1081376 | tf_op jit(solution)/shard_map/ppermute | solution.py:29
  208.7 0.1 fusion.78
  208.8 3.1 slice.116
  212.0 3.1 slice.139
  215.1 0.3 fusion.47
  215.5 1.7 fusion.8
  217.2 1.7 fusion.7
  218.9 1.8 fusion.6
  220.7 1.8 fusion.5
  222.5 1.7 fusion.4
  224.2 1.8 fusion.3
  226.0 1.8 fusion.2
  227.7 1.8 fusion.1
  229.5 1.7 fusion
  231.2 0.0 all-reduce.3.cloned.1.call-update
  231.2 0.0 all-to-all-done
  231.3 8.3 %copy.15 = bf16[256,2,9,512]{3,1,0,2:T(2,128)(2,1)} copy(bf16[256,2,9,512]{3,1,2,0:T(2,128)(2,1)} %all-to-all-done) | data formatting | bytes 9437184 | tf_op jit(solution)/shard_map/all_to_all | solution.py:46
  239.5 8.1 %reshape.9 = bf16[512,9,512]{2,0,1:T(8,128)(2,1)} reshape(bf16[256,2,9,512]{3,1,0,2:T(2,128)(2,1)} %copy.15) | data formatting | bytes 9437184 | tf_op jit(solution)/shard_map/reshape | solution.py:45
  247.6 0.0 copy-start
  247.6 1.9 fusion.36
  249.5 1.8 fusion.39
  251.3 0.0 copy-done
  251.3 0.7 fusion.42
  252.1 0.7 fusion.45
  252.8 0.8 fusion.49
  253.6 0.7 fusion.52
  254.3 0.7 fusion.33
  255.1 0.7 fusion.59
  255.8 1.2 add_add_fusion
  257.0 0.1 slice_bitcast_fusion
  257.1 0.6 collective-permute-start.5
  257.8 26.2 %collective-permute-done.5 = f32[2,256,512]{2,1,0:T(8,128)S(1)} collective-permute-done((f32[2,256,512]{2,1,0:T(8,128)S(1)}, f32[2,256,512]{2,1,0:T(8,128)S(1)}, u32[]{:S(2)}, u32[]{:S(2)}) %collective-permute-start.5) | collective-permute-done | bytes 1048608 | tf_op jit(solution)/shard_map/ppermute | solution.py:29
  284.0 0.0 collective-permute-start.6
  284.0 32.5 %collective-permute-done.6 = f32[2,256,512]{2,1,0:T(8,128)S(1)} collective-permute-done((f32[2,256,512]{2,1,0:T(8,128)S(1)}, f32[2,256,512]{2,1,0:T(8,128)S(1)}, u32[]{:S(2)}, u32[]{:S(2)}) %collective-permute-start.6) | collective-permute-done | bytes 1048608 | tf_op jit(solution)/shard_map/ppermute | solution.py:29
  316.5 0.0 collective-permute-start.7
  316.5 278.4 %all-reduce.3.cloned.1.call-done = f32[512,9,512]{2,0,1:T(8,128)} async-done(((f32[512,9,512]{2,0,1:T(8,128)}), f32[512,9,512]{2,0,1:T(8,128)}) %all-reduce.3.cloned.1.call-update) | async-done | bytes 9437200
  595.0 1.5 constant_dynamic-slice_fusion
  596.5 0.0 collective-permute-done.7
  596.5 7.5 %rev.6 = f32[2,256,512]{2,1,0:T(8,128)S(1)} reverse(f32[2,256,512]{2,1,0:T(8,128)} %collective-permute-done.7), dimensions={1,2} | reverse | bytes 2097152 | tf_op jit(solution)/shard_map/jit(_flip)/rev | solution.py:68
  604.0 1.0 fusion.56
  (1 shorter events, 0.0 us)
Async XLA Ops:
  12.5 15.3 %copy-start.2 = (bf16[2,256,512]{2,1,0:T(8,128)(2,1)S(1)}, bf16[2,256,512]{2,1,0:T(8,128)(2,1)}, u32[]{:S(2)}) copy-start(bf16[2,256,512]{2,1,0:T(8,128)(2,1)} %param.5) | copy-start | bytes 1572868
  12.5 15.3 %copy-start.3 = (bf16[2,256,512]{2,1,0:T(8,128)(2,1)S(1)}, bf16[2,256,512]{2,1,0:T(8,128)(2,1)}, u32[]{:S(2)}) copy-start(bf16[2,256,512]{2,1,0:T(8,128)(2,1)} %param.6) | copy-start | bytes 1572868
  12.5 15.8 %copy-start.1 = (bf16[2,256,512]{2,1,0:T(8,128)(2,1)S(1)}, bf16[2,256,512]{2,1,0:T(8,128)(2,1)}, u32[]{:S(2)}) copy-start(bf16[2,256,512]{2,1,0:T(8,128)(2,1)} %param.4) | copy-start | bytes 1572868
  12.5 218.7 %all-to-all-start = ((bf16[256,2,9,512]{3,1,2,0:T(2,128)(2,1)}), bf16[256,2,9,512]{3,1,2,0:T(2,128)(2,1)}, u32[]{:S(2)}, u32[]{:S(2)}) async-start(bf16[256,2,9,512]{3,1,2,0:T(2,128)(2,1)} %stack.36), calls=%async_computation | async-start | bytes 9437184 | tf_op jit(solution)/shard_map/all_to_all | solution.py:46
  27.8 567.2 %all-reduce.3.cloned.1.call-start = ((), (), s32[]{:S(2)}) async-start(), calls=%async_computation.1 | async-start | bytes 18874368
  28.4 6.9 %collective-permute-start = (bf16[2,2,4,512]{3,2,1,0:T(4,128)(2,1)S(1)}, bf16[2,2,4,512]{3,2,1,0:T(4,128)(2,1)S(1)}, u32[]{:S(2)}, u32[]{:S(2)}) collective-permute-start(bf16[2,2,4,512]{3,2,1,0:T(4,128)(2,1)S(1)} %get-tuple-element.6), channel_id=1, source_target_pairs={{0,1},{1,2},{2,3},{3,4},{4,5},{5,6},{6,7},{8,9},{9,10},{10,11},{11... | collective-permute-start | bytes 49160 | tf_op jit(solution)/shard_map/ppermute | solution.py:14
  31.5 8.0 %collective-permute-start.1 = (bf16[2,2,4,512]{3,2,1,0:T(4,128)(2,1)S(1)}, bf16[2,2,4,512]{3,2,1,0:T(4,128)(2,1)S(1)}, u32[]{:S(2)}, u32[]{:S(2)}) collective-permute-start(bf16[2,2,4,512]{3,2,1,0:T(4,128)(2,1)S(1)} %get-tuple-element.7), channel_id=1, source_target_pairs={{1,0},{2,1},{3,2},{4,3},{5,4},{6,5},{7,6},{9,8},{10,9},{11,10},{12... | collective-permute-start | bytes 49160 | tf_op jit(solution)/shard_map/ppermute | solution.py:17
  39.8 44.1 %collective-permute-start.2 = (bf16[2,2,264,512]{3,2,1,0:T(8,128)(2,1)S(1)}, bf16[2,2,264,512]{3,2,1,0:T(8,128)(2,1)S(1)}, u32[]{:S(2)}, u32[]{:S(2)}) collective-permute-start(bf16[2,2,264,512]{3,2,1,0:T(8,128)(2,1)S(1)} %pad_maximum_fusion), channel_id=1, source_target_pairs={{0,1},{1,0},{2,3},{3,2},{4,5},{5,4},{6,7},{7,6},{8,9},{9,8},{10,11... | collective-permute-start | bytes 3244040 | tf_op jit(solution)/shard_map/ppermute | solution.py:29
  83.8 97.1 %collective-permute-start.3 = (bf16[2,2,264,512]{3,2,1,0:T(8,128)(2,1)S(1)}, bf16[2,2,264,512]{3,2,1,0:T(8,128)(2,1)S(1)}, u32[]{:S(2)}, u32[]{:S(2)}) collective-permute-start(bf16[2,2,264,512]{3,2,1,0:T(8,128)(2,1)S(1)} %collective-permute-done.2), channel_id=1, source_target_pairs={{0,2},{2,0},{1,3},{3,1},{4,6},{6,4},{5,7},{7,5},{8,10},{10,8},{9,1... | collective-permute-start | bytes 3244040 | tf_op jit(solution)/shard_map/ppermute | solution.py:29
  180.9 27.8 %collective-permute-start.4 = (bf16[2,2,264,512]{3,2,1,0:T(8,128)(2,1)S(1)}, bf16[2,2,264,512]{3,2,1,0:T(8,128)(2,1)S(1)}, u32[]{:S(2)}, u32[]{:S(2)}) collective-permute-start(bf16[2,2,264,512]{3,2,1,0:T(8,128)(2,1)S(1)} %collective-permute-done.3), channel_id=1, source_target_pairs={{0,4},{4,0},{1,5},{5,1},{2,6},{6,2},{3,7},{7,3},{8,12},{12,8},{9,1... | collective-permute-start | bytes 3244040 | tf_op jit(solution)/shard_map/ppermute | solution.py:29
  247.6 3.7 copy-start
  257.1 26.9 %collective-permute-start.5 = (f32[2,256,512]{2,1,0:T(8,128)S(1)}, f32[2,256,512]{2,1,0:T(8,128)S(1)}, u32[]{:S(2)}, u32[]{:S(2)}) collective-permute-start(f32[2,256,512]{2,1,0:T(8,128)S(1)} %slice_bitcast_fusion), channel_id=1, source_target_pairs={{0,1},{1,0},{2,3},{3,2},{4,5},{5,4},{6,7},{7,6},{8,9},{9,8},{10,11... | collective-permute-start | bytes 3145736 | tf_op jit(solution)/shard_map/ppermute | solution.py:29
  284.0 32.5 %collective-permute-start.6 = (f32[2,256,512]{2,1,0:T(8,128)S(1)}, f32[2,256,512]{2,1,0:T(8,128)S(1)}, u32[]{:S(2)}, u32[]{:S(2)}) collective-permute-start(f32[2,256,512]{2,1,0:T(8,128)S(1)} %collective-permute-done.5), channel_id=1, source_target_pairs={{0,2},{2,0},{1,3},{3,1},{4,6},{6,4},{5,7},{7,5},{8,10},{10,8},{9,1... | collective-permute-start | bytes 3145736 | tf_op jit(solution)/shard_map/ppermute | solution.py:29
  316.5 280.0 %collective-permute-start.7 = (f32[2,256,512]{2,1,0:T(8,128)S(1)}, f32[2,256,512]{2,1,0:T(8,128)}, u32[]{:S(2)}, u32[]{:S(2)}) collective-permute-start(f32[2,256,512]{2,1,0:T(8,128)S(1)} %collective-permute-done.6), channel_id=1, source_target_pairs={{0,4},{4,0},{1,5},{5,1},{2,6},{6,2},{3,7},{7,3},{8,12},{12,8},{9,1... | collective-permute-start | bytes 3145736 | tf_op jit(solution)/shard_map/ppermute | solution.py:29
Sparse Core Ops, SparseCore 0:
  231.4 363.5 all-reduce.2
